TPU v7x, 512 devices: a whole 4x4x16 slice. The times are simulated.
512 devices in a mesh: dp: 512 (over x, z, y, core).
Axes of the slice: x: 4, y: 4, z: 16, core: 2. Of those that a mesh axis runs over, the one named last changes fastest.
Arguments:
- image_emb: bfloat16 [262144, 1152], P('dp'), may hold values from -0.71875 to 0.71875
- text_emb: bfloat16 [262144, 1152], P('dp'), may hold values from -0.71875 to 0.71875
- logit_scale: float32 [1], replicated, may hold values from 2 to 8
- logit_bias: float32 [1], replicated, may hold values from -3 to 0
Outputs:
- image_grad: bfloat16 [262144, 1152], P('dp')
- text_grad: bfloat16 [262144, 1152], P('dp')
- loss_rows: float32 [262144], P('dp')
All inputs are finite; a program needn't handle non-finite values.
Results may differ from a plain program's by a relative error of at most 0.005.
Values may be sent and summed in bfloat16 or wider, within the bound.
A program may use at most 64 MiB of HBM per device.

v0:
```python
import jax
import jax.numpy as jnp
from jax import lax
from jax.sharding import PartitionSpec as P


def passed_along(value, axis, steps):
    count = lax.axis_size(axis)
    pairs = [(source, (source + steps) % count) for source in range(count)]
    return lax.ppermute(value, axis, pairs)


def block_terms(images, texts, scale, bias, positive):
    logits = jnp.dot(images, texts.T, preferred_element_type=jnp.float32) * scale + bias
    count = logits.shape[0]
    rowpos = lax.broadcasted_iota(jnp.int32, (count, count), 0)
    colpos = lax.broadcasted_iota(jnp.int32, (count, count), 1)
    labels = (rowpos == colpos).astype(jnp.float32) * positive
    losses = jax.nn.softplus(logits) - labels * logits
    weights = ((jax.nn.sigmoid(logits) - labels) * scale).astype(jnp.bfloat16)
    return (jnp.sum(losses, axis=1), weights)


def text_partial(weights, images):
    return lax.dot_general(
        weights, images, (((0,), (0,)), ((), ())), preferred_element_type=jnp.float32
    )


def per_device(image_emb, text_emb, logit_scale, logit_bias):
    scale = logit_scale[0]
    bias = logit_bias[0]
    count = image_emb.shape[0]
    blocks = [text_emb]
    current = text_emb
    for step in range(2):
        current = passed_along(current, "dp", 1)
        blocks.append(current)
    loss_sum = jnp.zeros((count,), jnp.float32)
    grad_img = jnp.zeros(image_emb.shape, jnp.float32)
    partials = []
    for place in range(3):
        positive = 1.0 if place == 0 else 0.0
        losses, weights = block_terms(image_emb, blocks[place], scale, bias, positive)
        loss_sum = loss_sum + losses
        grad_img = grad_img + jnp.dot(weights, blocks[place], preferred_element_type=jnp.float32)
        partials.append(text_partial(weights, image_emb))
    first = partials[1].astype(jnp.bfloat16)
    second = partials[2].astype(jnp.bfloat16)
    home_one, carried = passed_along((first, second), "dp", -1)
    home_two = passed_along(carried, "dp", -1)
    total = partials[0] + home_one.astype(jnp.float32) + home_two.astype(jnp.float32)
    loss_rows = loss_sum / (3.0 * count)
    return (grad_img.astype(jnp.bfloat16), total.astype(jnp.bfloat16), loss_rows)


def solution(mesh):
    in_specs = (P("dp", None), P("dp", None), P(), P())
    out_specs = (P("dp", None), P("dp", None), P("dp"))
    return jax.shard_map(
        per_device, mesh=mesh, in_specs=in_specs, out_specs=out_specs, check_vma=False
    )
```

profile of v0, /device:TPU:1, one launch (start us, length us, event | category | flops | bytes accessed | tf_op | source)
XLA Modules:
  0.0 95.5 jit_solution(3072056247087853154)
XLA Ops:
  0.6 0.0 copy-start
  0.6 4.7 %collective-permute-start = (bf16[512,1152]{1,0:T(8,128)(2,1)}, bf16[512,1152]{1,0:T(8,128)(2,1)S(1)}, u32[]{:S(2)}, u32[]{:S(2)}) collective-permute-start(bf16[512,1152]{1,0:T(8,128)(2,1)} %param.5), channel_id=1, source_target_pairs={{0,1},{1,2},{2,3},{3,4},{4,5},{5,6},{6,7},{7,8},{8,9},{9,10},{10,1... | collective-permute-start | bytes 3538952 | tf_op jit(solution)/shard_map/ppermute | solution.py:10
  5.4 13.4 %collective-permute-done = bf16[512,1152]{1,0:T(8,128)(2,1)S(1)} collective-permute-done((bf16[512,1152]{1,0:T(8,128)(2,1)}, bf16[512,1152]{1,0:T(8,128)(2,1)S(1)}, u32[]{:S(2)}, u32[]{:S(2)}) %collective-permute-start) | collective-permute-done | bytes 1179680 | tf_op jit(solution)/shard_map/ppermute | solution.py:10
  18.8 4.3 %collective-permute-start.1 = (bf16[512,1152]{1,0:T(8,128)(2,1)S(1)}, bf16[512,1152]{1,0:T(8,128)(2,1)S(1)}, u32[]{:S(2)}, u32[]{:S(2)}) collective-permute-start(bf16[512,1152]{1,0:T(8,128)(2,1)S(1)} %collective-permute-done), channel_id=1, source_target_pairs={{0,1},{1,2},{2,3},{3,4},{4,5},{5,6},{6,7},{7,8},{8,9},{9,10},{10,1... | collective-permute-start | bytes 3538952 | tf_op jit(solution)/shard_map/ppermute | solution.py:10
  24.4 11.8 %collective-permute-done.1 = bf16[512,1152]{1,0:T(8,128)(2,1)S(1)} collective-permute-done((bf16[512,1152]{1,0:T(8,128)(2,1)S(1)}, bf16[512,1152]{1,0:T(8,128)(2,1)S(1)}, u32[]{:S(2)}, u32[]{:S(2)}) %collective-permute-start.1) | collective-permute-done | bytes 1179680 | tf_op jit(solution)/shard_map/ppermute | solution.py:10
  36.2 0.0 copy-done
  36.2 1.5 %fusion.9 = (f32[512]{0:T(512)S(1)}, f32[512,512]{0,1:T(8,128)S(1)}) fusion(f32[]{:T(128)} %bitcast.24, f32[]{:T(128)} %bitcast.16, bf16[512,1152]{1,0:T(8,128)(2,1)S(1)} %copy-done, bf16[512,1152]{1,0:T(8,128)(2,1)S(1)} %collective-permute-done.1), kind=kOutput, calls=%fused_computation.20 | convolution fusion | flops 606862848 | bytes 3409928 | tf_op jit(solution)/shard_map/dot_general | solution.py:14
  37.7 0.0 copy-start.1
  37.7 1.0 %convolution_convert_fusion = bf16[512,1152]{1,0:T(8,128)(2,1)S(1)} fusion(bf16[512,1152]{1,0:T(8,128)(2,1)S(1)} %copy-done, f32[512,512]{0,1:T(8,128)S(1)} %get-tuple-element.4, f32[]{:T(128)} %bitcast.21), kind=kOutput, calls=%fused_computation.6 | convolution fusion | flops 605880320 | bytes 3407876 | tf_op jit(solution)/shard_map/dot_general | solution.py:25
  38.7 20.5 %collective-permute-start.3 = (bf16[512,1152]{1,0:T(8,128)(2,1)S(1)}, bf16[512,1152]{1,0:T(8,128)(2,1)S(1)}, u32[]{:S(2)}, u32[]{:S(2)}) collective-permute-start(bf16[512,1152]{1,0:T(8,128)(2,1)S(1)} %convolution_convert_fusion), channel_id=1, source_target_pairs={{0,511},{1,0},{2,1},{3,2},{4,3},{5,4},{6,5},{7,6},{8,7},{9,8},{10,... | collective-permute-start | bytes 3538952 | tf_op jit(solution)/shard_map/ppermute | solution.py:10
  59.2 1.4 %fusion.5 = (f32[512]{0:T(512)S(1)}, f32[512,512]{0,1:T(8,128)S(1)}) fusion(f32[]{:T(128)} %bitcast.23, f32[]{:T(128)} %bitcast.14, bf16[512,1152]{1,0:T(8,128)(2,1)S(1)} %copy-done, bf16[512,1152]{1,0:T(8,128)(2,1)S(1)} %copy-done.1), kind=kOutput, calls=%fused_computation.16 | convolution fusion | flops 607124992 | bytes 3409928 | tf_op jit(solution)/shard_map/dot_general | solution.py:14
  60.6 0.9 fusion.11
  61.6 1.5 %fusion.7 = (f32[512]{0:T(512)S(1)}, f32[512,512]{0,1:T(8,128)S(1)}) fusion(f32[]{:T(128)} %bitcast.25, f32[]{:T(128)} %bitcast.18, bf16[512,1152]{1,0:T(8,128)(2,1)S(1)} %copy-done, bf16[512,1152]{1,0:T(8,128)(2,1)S(1)} %collective-permute-done), kind=kOutput, calls=%fused_computation.18 | convolution fusion | flops 606862848 | bytes 3409928 | tf_op jit(solution)/shard_map/dot_general | solution.py:14
  63.0 1.0 %convolution_convert_fusion.1 = bf16[512,1152]{1,0:T(8,128)(2,1)S(1)} fusion(bf16[512,1152]{1,0:T(8,128)(2,1)S(1)} %copy-done, f32[512,512]{0,1:T(8,128)S(1)} %get-tuple-element.8, f32[]{:T(128)} %bitcast.20), kind=kOutput, calls=%fused_computation.7 | convolution fusion | flops 605880320 | bytes 3407876 | tf_op jit(solution)/shard_map/dot_general | solution.py:25
  64.0 1.9 %collective-permute-start.2 = (bf16[512,1152]{1,0:T(8,128)(2,1)S(1)}, bf16[512,1152]{1,0:T(8,128)(2,1)S(1)}, u32[]{:S(2)}, u32[]{:S(2)}) collective-permute-start(bf16[512,1152]{1,0:T(8,128)(2,1)S(1)} %convolution_convert_fusion.1), channel_id=1, source_target_pairs={{0,511},{1,0},{2,1},{3,2},{4,3},{5,4},{6,5},{7,6},{8,7},{9,8},{10,... | collective-permute-start | bytes 3538952 | tf_op jit(solution)/shard_map/ppermute | solution.py:10
  65.9 0.0 collective-permute-done.3
  66.0 8.8 %collective-permute-start.4 = (bf16[512,1152]{1,0:T(8,128)(2,1)S(1)}, bf16[512,1152]{1,0:T(8,128)(2,1)S(1)}, u32[]{:S(2)}, u32[]{:S(2)}) collective-permute-start(bf16[512,1152]{1,0:T(8,128)(2,1)S(1)} %collective-permute-done.3), channel_id=1, source_target_pairs={{0,511},{1,0},{2,1},{3,2},{4,3},{5,4},{6,5},{7,6},{8,7},{9,8},{10,... | collective-permute-start | bytes 3538952 | tf_op jit(solution)/shard_map/ppermute | solution.py:10
  74.8 1.0 %fusion.10 = f32[512,1152]{1,0:T(8,128)S(1)} fusion(bf16[512,1152]{1,0:T(8,128)(2,1)S(1)} %copy-done, f32[512,512]{0,1:T(8,128)S(1)} %get-tuple-element.6, f32[]{:T(128)} %bitcast.22), kind=kOutput, calls=%fused_computation.26 | convolution fusion | flops 606076928 | bytes 4587524 | tf_op jit(solution)/shard_map/dot_general | solution.py:25
  75.8 0.9 convolution_add_fusion.1
  76.7 0.6 add_multiply_fusion
  77.3 2.0 %fusion = bf16[512,1152]{1,0:T(8,128)(2,1)} fusion(f32[512,1152]{1,0:T(8,128)S(1)} %convolution_add_fusion.1, bf16[512,1152]{1,0:T(8,128)(2,1)S(1)} %collective-permute-done.1, f32[512,512]{0,1:T(8,128)S(1)} %get-tuple-element.4, f32[]{:T(128)} %bitcast.15), kind=kOutput, calls=%fused_computation.5 | convolution fusion | flops 606470144 | bytes 5767172 | tf_op jit(solution)/shard_map/dot_general | solution.py:46
  79.3 2.3 %collective-permute-done.2 = bf16[512,1152]{1,0:T(8,128)(2,1)S(1)} collective-permute-done((bf16[512,1152]{1,0:T(8,128)(2,1)S(1)}, bf16[512,1152]{1,0:T(8,128)(2,1)S(1)}, u32[]{:S(2)}, u32[]{:S(2)}) %collective-permute-start.2) | collective-permute-done | bytes 1179680 | tf_op jit(solution)/shard_map/ppermute | solution.py:10
  81.5 12.6 %collective-permute-done.4 = bf16[512,1152]{1,0:T(8,128)(2,1)S(1)} collective-permute-done((bf16[512,1152]{1,0:T(8,128)(2,1)S(1)}, bf16[512,1152]{1,0:T(8,128)(2,1)S(1)}, u32[]{:S(2)}, u32[]{:S(2)}) %collective-permute-start.4) | collective-permute-done | bytes 1179680 | tf_op jit(solution)/shard_map/ppermute | solution.py:10
  94.2 1.4 %add_convert_fusion = bf16[512,1152]{1,0:T(8,128)(2,1)} fusion(bf16[512,1152]{1,0:T(8,128)(2,1)S(1)} %collective-permute-done.4, f32[512,1152]{1,0:T(8,128)S(1)} %fusion.10, bf16[512,1152]{1,0:T(8,128)(2,1)S(1)} %collective-permute-done.2), kind=kLoop, calls=%fused_computation.8 | loop fusion | flops 2949120 | bytes 5898240 | tf_op jit(solution)/shard_map/convert_element_type | solution.py:54
  (1 shorter events, 0.0 us)
Async XLA Ops:
  0.6 35.6 %copy-start = (bf16[512,1152]{1,0:T(8,128)(2,1)S(1)}, bf16[512,1152]{1,0:T(8,128)(2,1)}, u32[]{:S(2)}) copy-start(bf16[512,1152]{1,0:T(8,128)(2,1)} %param.4) | copy-start | bytes 3538948
  0.6 18.2 %collective-permute-start = (bf16[512,1152]{1,0:T(8,128)(2,1)}, bf16[512,1152]{1,0:T(8,128)(2,1)S(1)}, u32[]{:S(2)}, u32[]{:S(2)}) collective-permute-start(bf16[512,1152]{1,0:T(8,128)(2,1)} %param.5), channel_id=1, source_target_pairs={{0,1},{1,2},{2,3},{3,4},{4,5},{5,6},{6,7},{7,8},{8,9},{9,10},{10,1... | collective-permute-start | bytes 3538952 | tf_op jit(solution)/shard_map/ppermute | solution.py:10
  18.8 17.4 %collective-permute-start.1 = (bf16[512,1152]{1,0:T(8,128)(2,1)S(1)}, bf16[512,1152]{1,0:T(8,128)(2,1)S(1)}, u32[]{:S(2)}, u32[]{:S(2)}) collective-permute-start(bf16[512,1152]{1,0:T(8,128)(2,1)S(1)} %collective-permute-done), channel_id=1, source_target_pairs={{0,1},{1,2},{2,3},{3,4},{4,5},{5,6},{6,7},{7,8},{8,9},{9,10},{10,1... | collective-permute-start | bytes 3538952 | tf_op jit(solution)/shard_map/ppermute | solution.py:10
  37.7 21.5 %copy-start.1 = (bf16[512,1152]{1,0:T(8,128)(2,1)S(1)}, bf16[512,1152]{1,0:T(8,128)(2,1)}, u32[]{:S(2)}) copy-start(bf16[512,1152]{1,0:T(8,128)(2,1)} %param.5) | copy-start | bytes 3538948
  38.7 27.2 %collective-permute-start.3 = (bf16[512,1152]{1,0:T(8,128)(2,1)S(1)}, bf16[512,1152]{1,0:T(8,128)(2,1)S(1)}, u32[]{:S(2)}, u32[]{:S(2)}) collective-permute-start(bf16[512,1152]{1,0:T(8,128)(2,1)S(1)} %convolution_convert_fusion), channel_id=1, source_target_pairs={{0,511},{1,0},{2,1},{3,2},{4,3},{5,4},{6,5},{7,6},{8,7},{9,8},{10,... | collective-permute-start | bytes 3538952 | tf_op jit(solution)/shard_map/ppermute | solution.py:10
  64.0 17.5 %collective-permute-start.2 = (bf16[512,1152]{1,0:T(8,128)(2,1)S(1)}, bf16[512,1152]{1,0:T(8,128)(2,1)S(1)}, u32[]{:S(2)}, u32[]{:S(2)}) collective-permute-start(bf16[512,1152]{1,0:T(8,128)(2,1)S(1)} %convolution_convert_fusion.1), channel_id=1, source_target_pairs={{0,511},{1,0},{2,1},{3,2},{4,3},{5,4},{6,5},{7,6},{8,7},{9,8},{10,... | collective-permute-start | bytes 3538952 | tf_op jit(solution)/shard_map/ppermute | solution.py:10
  66.0 28.2 %collective-permute-start.4 = (bf16[512,1152]{1,0:T(8,128)(2,1)S(1)}, bf16[512,1152]{1,0:T(8,128)(2,1)S(1)}, u32[]{:S(2)}, u32[]{:S(2)}) collective-permute-start(bf16[512,1152]{1,0:T(8,128)(2,1)S(1)} %collective-permute-done.3), channel_id=1, source_target_pairs={{0,511},{1,0},{2,1},{3,2},{4,3},{5,4},{6,5},{7,6},{8,7},{9,8},{10,... | collective-permute-start | bytes 3538952 | tf_op jit(solution)/shard_map/ppermute | solution.py:10
where the time goes:
time: 95.8 us; the launch traced here: 95.5 us
  starting transfers between devices  40.2 us (42%)
  waiting for transfers between devices  40.2 us (42%)
  matrix products  11.1 us (12%)
  between operations  2.04 us (2%)
  other arithmetic  1.96 us (2%)
    ppermute x5, starting transfers between devices, passed_along(): return lax.ppermute(value, axis, pairs)  40.2 us
    ppermute x5, waiting for transfers between devices, passed_along(): return lax.ppermute(value, axis, pairs)  40.2 us
    dot_general x3, matrix products, block_terms(): jnp.dot(images, texts.T, preferred_element_type=jnp.float32) * scale + bias  4.38 us
    dot_general x3, matrix products, per_device(): jnp.dot(weights, blocks[place], preferred_element_type=jnp.float32)  3.81 us
    dot_general x3, matrix products, text_partial(): lax.dot_general(weights, images, (((0,), (0,)), ((), ())), preferred_elem...  2.93 us
  transfers between devices with their start and end apart: 5, of which 4 were waited for; matrix products, arithmetic and copies ran while one was open for 10% of the time, Pallas kernels for 0%

commit v1 on v0

v1 whole, which is shorter than its diff:
```python
import jax
import jax.numpy as jnp
from jax import lax
from jax.experimental import pallas as pl
from jax.experimental.pallas import tpu as pltpu
from jax.sharding import PartitionSpec as P

MESH = pl.DeviceIdType.MESH
CHUNKS = 4


def exchange_kernel(
    count,
    scale_ref,
    bias_ref,
    image_ref,
    text_ref,
    grad_ref,
    loss_ref,
    own,
    early,
    first,
    second,
    passed,
    total,
    logs,
    lins,
    own_sem,
    early_sem,
    first_sem,
    second_sem,
    passed_sem,
    ready_sem,
):
    rows, depth = image_ref.shape
    step = rows // CHUNKS
    me = lax.axis_index("dp")
    odd = lax.rem(me, 2)
    even = 1 - odd
    other = me + 1 - 2 * odd
    ahead = lax.rem(me + 2, count)
    behind = lax.rem(me + count - 2, count)

    barrier = pltpu.get_barrier_semaphore()
    for device in (behind, other):
        pl.semaphore_signal(barrier, inc=1, device_id=(device,), device_id_type=MESH)

    loads = []
    for place, ref in ((0, image_ref), (1, text_ref)):
        load = pltpu.make_async_copy(ref, own.at[place], own_sem.at[place])
        load.start()
        loads.append(load)

    def part(index):
        return pl.ds(index * step, step)

    def send(source, target, sems, index, device):
        return pltpu.make_async_remote_copy(
            src_ref=source.at[part(index)],
            dst_ref=target.at[part(index)],
            send_sem=sems.at[0, index],
            recv_sem=sems.at[1, index],
            device_id=(device,),
            device_id_type=MESH,
        )

    texts_first = [send(own.at[1], first, first_sem, c, ahead) for c in range(CHUNKS)]
    texts_second = [send(own.at[1], second, second_sem, c, ahead) for c in range(CHUNKS)]
    images_first = [send(own.at[0], first, first_sem, c, behind) for c in range(CHUNKS)]
    images_second = [send(own.at[0], second, second_sem, c, behind) for c in range(CHUNKS)]
    to_other = pltpu.make_async_remote_copy(
        src_ref=own.at[even],
        dst_ref=early,
        send_sem=early_sem.at[0],
        recv_sem=early_sem.at[1],
        device_id=(other,),
        device_id_type=MESH,
    )
    onward = [send(first, passed, passed_sem, c, other) for c in range(CHUNKS)]

    total[...] = jnp.zeros_like(total)
    logs[...] = jnp.zeros_like(logs)
    lins[...] = jnp.zeros_like(lins)
    for load in loads:
        load.wait()
    pl.semaphore_wait(barrier, 2)
    pl.semaphore_signal(ready_sem, inc=1, device_id=(ahead,), device_id_type=MESH)

    @pl.when(odd == 1)
    def _():
        for copy in texts_first:
            copy.start()

    @pl.when(odd == 0)
    def _():
        for copy in texts_second:
            copy.start()

    to_other.start()
    pl.semaphore_wait(ready_sem, 1)

    @pl.when(odd == 1)
    def _():
        for copy in images_second:
            copy.start()

    @pl.when(odd == 0)
    def _():
        for copy in images_first:
            copy.start()

    scale = scale_ref[0]
    bias = bias_ref[0]

    def weigh(side, block, base=None):
        logits = (
            lax.dot_general(
                own[side], block, (((1,), (1,)), ((), ())), preferred_element_type=jnp.float32
            )
            * scale
            + bias
        )
        small = jnp.exp(-jnp.abs(logits))
        below = 1.0 + small
        positive = logits >= 0.0
        sigmoid = jnp.where(positive, 1.0, small) / below
        linear = jnp.maximum(logits, 0.0)
        if base is not None:
            row = lax.broadcasted_iota(jnp.int32, logits.shape, 0)
            column = lax.broadcasted_iota(jnp.int32, logits.shape, 1) + base
            label = row == column
            linear = jnp.where(label, linear - logits, linear)
            sigmoid = jnp.where(label, sigmoid - 1.0, sigmoid)
        for lane in range(0, logits.shape[1], 128):
            here = slice(lane, lane + 128)
            logs[side] = logs[side] * below[:, here] + small[:, here]
            lins[side] += linear[:, here]
        return (sigmoid * scale).astype(jnp.bfloat16)

    def add(side, block):
        weights = weigh(side, block)
        total[side] += jnp.dot(weights, block, preferred_element_type=jnp.float32)

    for c in range(CHUNKS):
        block = own[1, part(c)]
        weights = weigh(0, block, c * step)
        total[0] += jnp.dot(weights, block, preferred_element_type=jnp.float32)
        total[1, part(c)] += lax.dot_general(
            weights, own[0], (((0,), (0,)), ((), ())), preferred_element_type=jnp.float32
        )

    to_other.wait_recv()
    for c in range(CHUNKS):
        add(even, early[part(c)])

    for c in range(CHUNKS):
        onward_in = onward[c]
        texts_first[c].wait_recv()
        onward[c].start()
        add(even, first[part(c)])
        texts_second[c].wait_recv()
        add(odd, second[part(c)])
        onward[c].wait_recv()
        add(odd, passed[part(c)])

    grad_ref[...] = total[...].astype(jnp.bfloat16)
    loss_ref[...] = lins[0] + jnp.log1p(logs[0])

    to_other.wait_send()
    for c in range(CHUNKS):
        texts_first[c].wait_send()
        texts_second[c].wait_send()
        onward[c].wait_send()


def per_device(count, image_emb, text_emb, logit_scale, logit_bias):
    rows, depth = image_emb.shape
    block = pltpu.VMEM((rows, depth), jnp.bfloat16)
    pair = pltpu.SemaphoreType.DMA((2, CHUNKS))
    grads, losses = pl.pallas_call(
        lambda *refs: exchange_kernel(count, *refs),
        out_shape=(
            jax.ShapeDtypeStruct((2, rows, depth), jnp.bfloat16),
            jax.ShapeDtypeStruct((rows, 128), jnp.float32),
        ),
        in_specs=[pl.BlockSpec(memory_space=pltpu.SMEM)] * 2
        + [pl.BlockSpec(memory_space=pl.ANY)] * 2,
        out_specs=[pl.BlockSpec(memory_space=pltpu.VMEM)] * 2,
        scratch_shapes=[
            pltpu.VMEM((2, rows, depth), jnp.bfloat16),
            block,
            block,
            block,
            block,
            pltpu.VMEM((2, rows, depth), jnp.float32),
            pltpu.VMEM((2, rows, 128), jnp.float32),
            pltpu.VMEM((2, rows, 128), jnp.float32),
            pltpu.SemaphoreType.DMA((2,)),
            pltpu.SemaphoreType.DMA((2,)),
            pair,
            pair,
            pair,
            pltpu.SemaphoreType.REGULAR,
        ],
        compiler_params=pltpu.CompilerParams(
            collective_id=0, has_side_effects=True, vmem_limit_bytes=56 << 20
        ),
        cost_estimate=pl.CostEstimate(
            flops=22 * rows * rows * depth, bytes_accessed=8 * rows * depth, transcendentals=0
        ),
    )(logit_scale, logit_bias, image_emb, text_emb)
    loss_rows = jnp.sum(losses, axis=1) / (3.0 * rows)
    return grads[0], grads[1], loss_rows


def solution(mesh):
    count = mesh.shape["dp"]
    in_specs = (P("dp", None), P("dp", None), P(), P())
    out_specs = (P("dp", None), P("dp", None), P("dp"))
    return jax.shard_map(
        lambda *arrays: per_device(count, *arrays),
        mesh=mesh,
        in_specs=in_specs,
        out_specs=out_specs,
        check_vma=False,
    )
```

time: 95.8 us -> 55.2 us (0.58)
  Pallas kernels: 0 us -> 49.1 us
  starting transfers between devices: 40.2 us -> 0 us
  waiting for transfers between devices: 40.2 us -> 0 us
  matrix products: 11.1 us -> 0 us
  local copies, waits for them, and re-layouts: 0.02 us -> 3.25 us
  other arithmetic: 1.96 us -> 0.73 us
    pallas_call x0 -> x1, Pallas kernels: none -> 49.1 us  [per_device(): pl.pallas_call(lambda *refs: exchange_kernel(count, *refs), out_shape=(ja...]
    ppermute x5 -> x0, starting transfers between devices: 40.2 us -> none  [passed_along(): return lax.ppermute(value, axis, pairs)]
    ppermute x5 -> x0, waiting for transfers between devices: 40.2 us -> none  [passed_along(): return lax.ppermute(value, axis, pairs)]
    dot_general x9 -> x0, matrix products: 11.1 us -> none  [the longest x3 4.38 us: block_terms(): jnp.dot(images, texts.T, preferred_element_type=jnp.float32) * scale + bias]
    squeeze x0 -> x1, local copies, waits for them, and re-layouts: none -> 3.25 us  [per_device(): return (grads[0], grads[1], loss_rows)]
    convert_element_type x1 -> x0, other arithmetic: 1.37 us -> none  [per_device(): total.astype(jnp.bfloat16)]
  transfers between devices with their start and end apart: 5 -> 0, of which waited for: 4 -> 0; matrix products, arithmetic and copies ran while one was open for 10% -> 0% of each run, Pallas kernels for 0% -> 0%
where the time goes in v1:
time: 55.2 us; the launch traced here: 55 us
  Pallas kernels  49.1 us (89%)
  local copies, waits for them, and re-layouts  3.25 us (6%)
  between operations  1.94 us (4%)
  other arithmetic  0.73 us (1%)
    pallas_call x1, Pallas kernels, per_device(): pl.pallas_call(lambda *refs: exchange_kernel(count, *refs), out_shape=(ja...  49.1 us
    squeeze x1, local copies, waits for them, and re-layouts, per_device(): return (grads[0], grads[1], loss_rows)  3.25 us

profile of v1, /device:TPU:1, one launch (start us, length us, event | category | flops | bytes accessed | tf_op | source)
XLA Modules:
  0.0 55.0 jit_solution(12523987834778816882)
XLA Ops:
  1.9 49.1 %shard_map.67 = (bf16[2,512,1152]{2,1,0:T(8,128)(2,1)}, f32[512,128]{1,0:T(8,128)}) custom-call(f32[1]{0:T(128)S(6)} %copy.7.refs_0_, f32[1]{0:T(128)S(6)} %copy.8.refs_1_, bf16[512,1152]{1,0:T(8,128)(2,1)} %refs_2_.1, bf16[512,1152]{1,0:T(8,128)(2,1)} %refs_3_.1), custom_call_target="tpu_custom_call" | custom-call | flops 6643777536 | bytes 4718592 | tf_op jit(solution)/shard_map/pallas_call | solution.py:180
  51.0 0.0 copy-start
  51.0 3.3 %slice_bitcast_fusion = (bf16[512,1152]{1,0:T(8,128)(2,1)}, bf16[512,1152]{1,0:T(8,128)(2,1)}) fusion(bf16[2,512,1152]{2,1,0:T(8,128)(2,1)} %get-tuple-element.5), kind=kLoop, calls=%fused_computation | loop fusion | bytes 4718592 | tf_op jit(solution)/shard_map/squeeze | solution.py:213
  54.3 0.0 copy-done
  54.3 0.1 reduce_sum.9
  54.4 0.6 %broadcast_multiply_fusion = f32[512]{0:T(512)} fusion(f32[512]{0:T(512)S(1)} %reduce_sum.9), kind=kLoop, calls=%fused_computation.2 | loop fusion | flops 512 | bytes 4096 | tf_op jit(solution)/shard_map/div | solution.py:212
Async XLA Ops:
  51.0 3.3 %copy-start = (f32[512,128]{1,0:T(8,128)S(1)}, f32[512,128]{1,0:T(8,128)}, u32[]{:S(2)}) copy-start(f32[512,128]{1,0:T(8,128)} %get-tuple-element.6) | copy-start | bytes 786436

commit v2 on v1

v2 whole, which is shorter than its diff:
```python
import jax
import jax.numpy as jnp
from jax import lax
from jax.experimental import pallas as pl
from jax.experimental.pallas import tpu as pltpu
from jax.sharding import PartitionSpec as P

MESH = pl.DeviceIdType.MESH
WIDE, NARROW, TAIL = 128, 64, 2
PIECES = 16
LOG2E = 1.4426950408889634


def exchange_kernel(
    count,
    scale_ref,
    bias_ref,
    image_ref,
    text_ref,
    total,
    logs,
    lins,
    own,
    early,
    first,
    late,
    own_sem,
    early_sem,
    first_sem,
    second_sem,
    passed_sem,
    ready_sem,
):
    rows, depth = image_ref.shape
    wide = (rows - NARROW * TAIL) // WIDE
    me = lax.axis_index("dp")
    odd = lax.rem(me, 2)
    even = 1 - odd
    other = me + 1 - 2 * odd
    ahead = lax.rem(me + 2, count)
    behind = lax.rem(me + count - 2, count)

    barrier = pltpu.get_barrier_semaphore()
    for device in (behind, other):
        pl.semaphore_signal(barrier, inc=1, device_id=(device,), device_id_type=MESH)

    loads = []
    for place, ref in ((0, image_ref), (1, text_ref)):
        load = pltpu.make_async_copy(ref, own.at[place], own_sem.at[place])
        load.start()
        loads.append(load)

    def span(index, narrow):
        if narrow:
            start = wide * WIDE + index * NARROW
            return pl.ds(start, NARROW), wide + index
        return pl.ds(pl.multiple_of(index * WIDE, WIDE), WIDE), index

    def send(source, target, sems, where, device, place=None):
        here, index = where
        there = here
        if place is not None:
            there = pl.ds(2 * here.start + place * here.size, here.size)
        return pltpu.make_async_remote_copy(
            src_ref=source.at[here],
            dst_ref=target.at[there],
            send_sem=sems.at[0, index],
            recv_sem=sems.at[1, index],
            device_id=(device,),
            device_id_type=MESH,
        )

    pieces = [span(c, False) for c in range(wide)] + [span(c, True) for c in range(TAIL)]

    def start_all(source, target, sems, device, place=None):
        for where in pieces:
            send(source, target, sems, where, device, place).start()

    to_other = pltpu.make_async_remote_copy(
        src_ref=own.at[even],
        dst_ref=early,
        send_sem=early_sem.at[0],
        recv_sem=early_sem.at[1],
        device_id=(other,),
        device_id_type=MESH,
    )

    total[...] = jnp.zeros_like(total)
    logs[...] = jnp.zeros_like(logs)
    lins[...] = jnp.zeros_like(lins)
    for load in loads:
        load.wait()
    pl.semaphore_wait(barrier, 2)

    @pl.when(odd == 1)
    def _():
        start_all(own.at[1], first, first_sem, ahead)

    pl.semaphore_signal(ready_sem, inc=1, device_id=(ahead,), device_id_type=MESH)
    to_other.start()

    @pl.when(odd == 0)
    def _():
        pl.semaphore_wait(ready_sem, 1)
        start_all(own.at[0], first, first_sem, behind)

    scale = scale_ref[0]
    slope = scale * LOG2E
    shift = bias_ref[0] * LOG2E

    halves = [pl.ds(0, rows // 2), pl.ds(rows // 2, rows // 2)]

    def weigh(side, half, block, base=None):
        logits = (
            lax.dot_general(
                own[side, half], block, (((1,), (1,)), ((), ())), preferred_element_type=jnp.float32
            )
            * slope
            + shift
        )
        small = jnp.exp2(jnp.minimum(logits, -logits))
        below = 1.0 + small
        positive = logits >= 0.0
        linear = jnp.maximum(logits, 0.0)
        if base is None:
            weights = jnp.where(positive, scale, scale * small)
        else:
            row = lax.broadcasted_iota(jnp.int32, logits.shape, 0) + half.start
            column = lax.broadcasted_iota(jnp.int32, logits.shape, 1) + base
            label = row == column
            linear = jnp.where(label, linear - logits, linear)
            weights = jnp.where(
                label,
                jnp.where(positive, -scale * small, -scale),
                jnp.where(positive, scale, scale * small),
            )
        width = min(logits.shape[1], 128)
        for lane in range(0, logits.shape[1], width):
            here = slice(lane, lane + width)
            logs[side, half, :width] = logs[side, half, :width] * below[:, here] + small[:, here]
            lins[side, half, :width] += linear[:, here]
        return (weights * pltpu.reciprocal(below, approx=True)).astype(jnp.bfloat16)

    def add(side, block):
        weights = [weigh(side, half, block) for half in halves]
        for half, factor in zip(halves, weights):
            total[side, half] += jnp.dot(factor, block, preferred_element_type=jnp.float32)

    @pl.loop(0, rows // 256)
    def _(c):
        here = pl.ds(pl.multiple_of(c * 256, 256), 256)
        block = own[1, here]
        weights = [weigh(0, half, block, c * 256) for half in halves]
        for half, factor in zip(halves, weights):
            total[0, half] += jnp.dot(factor, block, preferred_element_type=jnp.float32)
        total[1, here] += sum(
            lax.dot_general(
                factor, own[0, half], (((0,), (0,)), ((), ())), preferred_element_type=jnp.float32
            )
            for half, factor in zip(halves, weights)
        )

    send(own.at[odd], first, first_sem, pieces[0], other).wait_send()

    @pl.when(odd == 1)
    def _():
        pl.semaphore_wait(ready_sem, 1)
        start_all(own.at[0], late, second_sem, behind, 0)

    @pl.when(odd == 0)
    def _():
        start_all(own.at[1], late, second_sem, ahead, 0)

    to_other.wait_recv()

    @pl.loop(0, rows // 256)
    def _(c):
        add(even, early[pl.ds(pl.multiple_of(c * 256, 256), 256)])

    def turn(index, narrow):
        where = span(index, narrow)
        here = where[0]
        onward = send(first, late, passed_sem, where, other, 1)
        send(first, first, first_sem, where, other).wait_recv()
        onward.start()
        add(even, first[here])
        onward.wait_recv()
        send(own.at[0], late, second_sem, where, other, 0).wait_recv()
        add(odd, late[pl.ds(2 * here.start, 2 * here.size)])

    pl.loop(0, wide)(lambda c: turn(c, False))
    for c in range(TAIL):
        turn(c, True)

    to_other.wait_send()
    for where in pieces[1:]:
        send(own.at[0], first, first_sem, where, other).wait_send()
    for where in pieces:
        send(own.at[0], late, second_sem, where, other, 0).wait_send()
        send(first, late, passed_sem, where, other, 1).wait_send()


def finish_kernel(total, logs, lins, image_out, text_out, loss_out, held, loss, sems, loss_sem):
    rows = held.shape[1]
    step = rows // PIECES
    copies = []
    for place, out in ((0, image_out), (1, text_out)):
        for c in range(PIECES):
            here = pl.ds(c * step, step)
            held[place, here] = total[place, here].astype(jnp.bfloat16)
            copy = pltpu.make_async_copy(held.at[place, here], out.at[here], sems.at[place, c])
            copy.start()
            copies.append(copy)
    sums = lins[0] * (1.0 / LOG2E) + jnp.log1p(logs[0])
    loss[...] = jnp.sum(sums.T, axis=0) / (3.0 * rows)
    last = pltpu.make_async_copy(loss, loss_out, loss_sem)
    last.start()
    for copy in copies:
        copy.wait()
    last.wait()


def per_device(count, image_emb, text_emb, logit_scale, logit_bias):
    rows, depth = image_emb.shape
    inputs = [pltpu.with_memory_space_constraint(x, pltpu.HBM) for x in (image_emb, text_emb)]
    block = pltpu.VMEM((rows, depth), jnp.bfloat16)
    pieces = (rows - NARROW * TAIL) // WIDE + TAIL
    pair = pltpu.SemaphoreType.DMA((2, pieces))
    totals = pl.pallas_call(
        lambda *refs: exchange_kernel(count, *refs),
        out_shape=(
            pltpu.VMEM((2, rows, depth), jnp.float32),
            pltpu.VMEM((2, rows, 128), jnp.float32),
            pltpu.VMEM((2, rows, 128), jnp.float32),
        ),
        in_specs=[pl.BlockSpec(memory_space=pltpu.SMEM)] * 2
        + [pl.BlockSpec(memory_space=pltpu.HBM)] * 2,
        out_specs=[pl.BlockSpec(memory_space=pltpu.VMEM)] * 3,
        scratch_shapes=[
            pltpu.VMEM((2, rows, depth), jnp.bfloat16),
            block,
            block,
            pltpu.VMEM((2 * rows, depth), jnp.bfloat16),
            pltpu.SemaphoreType.DMA((2,)),
            pltpu.SemaphoreType.DMA((2,)),
            pair,
            pair,
            pair,
            pltpu.SemaphoreType.REGULAR,
        ],
        compiler_params=pltpu.CompilerParams(
            collective_id=0, has_side_effects=True, vmem_limit_bytes=40 << 20
        ),
        cost_estimate=pl.CostEstimate(
            flops=22 * rows * rows * depth, bytes_accessed=8 * rows * depth, transcendentals=0
        ),
    )(logit_scale, logit_bias, *inputs)
    return pl.pallas_call(
        finish_kernel,
        out_shape=(
            jax.ShapeDtypeStruct((rows, depth), jnp.bfloat16),
            jax.ShapeDtypeStruct((rows, depth), jnp.bfloat16),
            jax.ShapeDtypeStruct((rows,), jnp.float32),
        ),
        in_specs=[pl.BlockSpec(memory_space=pltpu.VMEM)] * 3,
        out_specs=[pl.BlockSpec(memory_space=pl.ANY)] * 3,
        scratch_shapes=[
            pltpu.VMEM((2, rows, depth), jnp.bfloat16),
            pltpu.VMEM((rows,), jnp.float32),
            pltpu.SemaphoreType.DMA((2, PIECES)),
            pltpu.SemaphoreType.DMA,
        ],
        compiler_params=pltpu.CompilerParams(vmem_limit_bytes=16 << 20),
    )(*totals)


def solution(mesh):
    count = mesh.shape["dp"]
    in_specs = (P("dp", None), P("dp", None), P(), P())
    out_specs = (P("dp", None), P("dp", None), P("dp"))
    return jax.shard_map(
        lambda *arrays: per_device(count, *arrays),
        mesh=mesh,
        in_specs=in_specs,
        out_specs=out_specs,
        check_vma=False,
    )
```

time: 55.2 us -> 49.6 us (0.90)
  local copies, waits for them, and re-layouts: 3.25 us -> 0 us
  Pallas kernels: 49.1 us -> 47.5 us
  other arithmetic: 0.73 us -> 0 us
    squeeze x1 -> x0, local copies, waits for them, and re-layouts: 3.25 us -> none  [per_device(): return (grads[0], grads[1], loss_rows)]
    pallas_call x1 -> x2, Pallas kernels: 49.1 us -> 47.5 us  [the longest x1 45.7 us: per_device(): pl.pallas_call(lambda *refs: exchange_kernel(count, *refs), out_shape=(pl...]
    div x1 -> x0, other arithmetic: 0.58 us -> none  [per_device(): loss_rows = jnp.sum(losses, axis=1) / (3.0 * rows)]
where the time goes in v2:
time: 49.6 us; the launch traced here: 49.4 us
  Pallas kernels  47.5 us (96%)
  between operations  1.93 us (4%)
    pallas_call x1, Pallas kernels, per_device(): pl.pallas_call(lambda *refs: exchange_kernel(count, *refs), out_shape=(pl...  45.7 us
    pallas_call x1, Pallas kernels, per_device(): pl.pallas_call(finish_kernel, out_shape=(jax.ShapeDtypeStruct((rows, dept...  1.79 us

profile of v2, /device:TPU:1, one launch (start us, length us, event | category | flops | bytes accessed | tf_op | source)
XLA Modules:
  0.0 49.4 jit_solution(14509668392698351828)
XLA Ops:
  1.9 45.7 %shard_map.67 = (f32[2,512,1152]{2,1,0:T(8,128)S(1)}, f32[2,512,128]{2,1,0:T(8,128)S(1)}, f32[2,512,128]{2,1,0:T(8,128)S(1)}) custom-call(f32[1]{0:T(128)S(6)} %copy.7.refs_0_, f32[1]{0:T(128)S(6)} %copy.8.refs_1_, bf16[512,1152]{1,0:T(8,128)(2,1)} %refs_2_.1, bf16[512,1152]{1,0:T(8,128)(2,1)} %refs_3_.1), custom_call_target="tpu_custom_call" | custom-call | flops 6643777536 | bytes 4718592 | tf_op jit(solution)/shard_map/pallas_call | solution.py:229
  47.6 1.8 %shard_map.68 = (bf16[512,1152]{1,0:T(8,128)(2,1)}, bf16[512,1152]{1,0:T(8,128)(2,1)}, f32[512]{0:T(512)}) custom-call(f32[2,512,1152]{2,1,0:T(8,128)S(1)} %get-tuple-element.6.total, f32[2,512,128]{2,1,0:T(8,128)S(1)} %get-tuple-element.7.logs, f32[2,512,128]{2,1,0:T(8,128)S(1)} %get-tuple-element.8.lins), custom_call_target="tpu_custom_call" | custom-call | tf_op jit(solution)/shard_map/pallas_call | solution.py:258

commit v3 on v2

--- a/solution.py
+++ b/solution.py
@@ -8,6 +8,9 @@
 MESH = pl.DeviceIdType.MESH
 WIDE, NARROW, TAIL = 128, 64, 2
 PIECES = 16
+PLANE = 128
+RELAYS = ((0, 104), (1, 112))
+HEAD_START = 1
 LOG2E = 1.4426950408889634
 
 
@@ -23,13 +26,16 @@
     own,
     early,
     first,
+    relayed,
     late,
     own_sem,
     early_sem,
     first_sem,
     second_sem,
     passed_sem,
+    relay_sem,
     ready_sem,
+    other_sem,
 ):
     rows, depth = image_ref.shape
     wide = (rows - NARROW * TAIL) // WIDE
@@ -40,13 +46,40 @@
     ahead = lax.rem(me + 2, count)
     behind = lax.rem(me + count - 2, count)
 
+    place = lax.rem(me, PLANE)
+    is_head = place < 2
+    is_tail = place >= PLANE - 2
+    even_head = place == 0
+    even_tail = place == PLANE - 2
+    is_relay = [place == there for _, there in RELAYS]
+
+    def tell(semaphore, device):
+        pl.semaphore_signal(semaphore, inc=1, device_id=(device,), device_id_type=MESH)
+
     barrier = pltpu.get_barrier_semaphore()
-    for device in (behind, other):
-        pl.semaphore_signal(barrier, inc=1, device_id=(device,), device_id_type=MESH)
+    tell(barrier, behind)
+
+    @pl.when(odd == 1)
+    def _():
+        tell(barrier, other)
+
+    @pl.when(even_head)
+    def _():
+        for _, there in RELAYS:
+            tell(barrier, lax.rem(me - PLANE + there + count, count))
+
+    for chosen, (_, there) in zip(is_relay, RELAYS):
+
+        @pl.when(chosen)
+        def _(there=there):
+            tell(barrier, me - there + PLANE - 2)
+
+    heard = 1 + even + jnp.where(even_tail, len(RELAYS), 0)
+    heard += sum(jnp.where(chosen, 1, 0) for chosen in is_relay)
 
     loads = []
-    for place, ref in ((0, image_ref), (1, text_ref)):
-        load = pltpu.make_async_copy(ref, own.at[place], own_sem.at[place])
+    for side, ref in ((0, image_ref), (1, text_ref)):
+        load = pltpu.make_async_copy(ref, own.at[side], own_sem.at[side])
         load.start()
         loads.append(load)
 
@@ -54,7 +87,10 @@
         if narrow:
             start = wide * WIDE + index * NARROW
             return pl.ds(start, NARROW), wide + index
-        return pl.ds(pl.multiple_of(index * WIDE, WIDE), WIDE), index
+        start = index * WIDE
+        if not isinstance(index, int):
+            start = pl.multiple_of(start, WIDE)
+        return pl.ds(start, WIDE), index
 
     def send(source, target, sems, where, device, place=None):
         here, index = where
@@ -76,6 +112,28 @@
         for where in pieces:
             send(source, target, sems, where, device, place).start()
 
+    def to_relay(piece, there):
+        here, index = pieces[piece]
+        return pltpu.make_async_remote_copy(
+            src_ref=text_ref.at[here],
+            dst_ref=relayed.at[pl.ds(0, here.size)],
+            send_sem=second_sem.at[0, index],
+            recv_sem=relay_sem.at[1],
+            device_id=(me - (PLANE - 2) + there,),
+            device_id_type=MESH,
+        )
+
+    def from_relay(piece, there):
+        here, index = pieces[piece]
+        return pltpu.make_async_remote_copy(
+            src_ref=relayed.at[pl.ds(0, here.size)],
+            dst_ref=late.at[pl.ds(2 * here.start, here.size)],
+            send_sem=relay_sem.at[0],
+            recv_sem=second_sem.at[1, index],
+            device_id=(lax.rem(me - there + PLANE, count),),
+            device_id_type=MESH,
+        )
+
     to_other = pltpu.make_async_remote_copy(
         src_ref=own.at[even],
         dst_ref=early,
@@ -85,24 +143,46 @@
         device_id_type=MESH,
     )
 
+    pl.semaphore_wait(barrier, heard)
+    tell(ready_sem, ahead)
+
+    neither = jnp.logical_and(place > 0, place < PLANE - 2)
+    early_ready = jnp.logical_not(is_head)
+
+    @pl.when(odd == 1)
+    def _():
+        start_all(text_ref, first, first_sem, ahead)
+
+    @pl.when(even_head)
+    def _():
+        start_all(text_ref, late, second_sem, ahead, 0)
+
+    @pl.when(even_tail)
+    def _():
+        for piece, there in RELAYS:
+            to_relay(piece, there).start()
+
+    @pl.when(odd == 0)
+    def _():
+        tell(other_sem, other)
+
     total[...] = jnp.zeros_like(total)
     logs[...] = jnp.zeros_like(logs)
     lins[...] = jnp.zeros_like(lins)
+
+    @pl.when(jnp.logical_and(even == 1, early_ready))
+    def _():
+        pl.semaphore_wait(ready_sem, 1)
+        start_all(image_ref, first, first_sem, behind)
+
     for load in loads:
         load.wait()
-    pl.semaphore_wait(barrier, 2)
 
     @pl.when(odd == 1)
     def _():
-        start_all(own.at[1], first, first_sem, ahead)
-
-    pl.semaphore_signal(ready_sem, inc=1, device_id=(ahead,), device_id_type=MESH)
+        pl.semaphore_wait(other_sem, 1)
+
     to_other.start()
-
-    @pl.when(odd == 0)
-    def _():
-        pl.semaphore_wait(ready_sem, 1)
-        start_all(own.at[0], first, first_sem, behind)
 
     scale = scale_ref[0]
     slope = scale * LOG2E
@@ -160,39 +240,96 @@
             for half, factor in zip(halves, weights)
         )
 
-    send(own.at[odd], first, first_sem, pieces[0], other).wait_send()
-
-    @pl.when(odd == 1)
+    started = jnp.logical_or(odd == 1, early_ready)
+
+    @pl.when(started)
+    def _():
+        send(own.at[odd], first, first_sem, pieces[0], other).wait_send()
+
+    @pl.when(jnp.logical_and(odd == 1, early_ready))
     def _():
         pl.semaphore_wait(ready_sem, 1)
-        start_all(own.at[0], late, second_sem, behind, 0)
-
-    @pl.when(odd == 0)
-    def _():
-        start_all(own.at[1], late, second_sem, ahead, 0)
+        start_all(image_ref, late, second_sem, behind, 0)
+
+    @pl.when(jnp.logical_and(even == 1, neither))
+    def _():
+        start_all(text_ref, late, second_sem, ahead, 0)
+
+    for chosen, (piece, there) in zip(is_relay, RELAYS):
+
+        @pl.when(chosen)
+        def _(piece=piece, there=there):
+            to_relay(piece, there).wait_recv()
+            from_relay(piece, there).start()
 
     to_other.wait_recv()
 
     @pl.loop(0, rows // 256)
     def _(c):
         add(even, early[pl.ds(pl.multiple_of(c * 256, 256), 256)])
+
+    @pl.when(even_tail)
+    def _():
+        for piece, where in enumerate(pieces):
+            if piece not in [index for index, _ in RELAYS]:
+                send(text_ref, late, second_sem, where, ahead, 0).start()
+
+    @pl.when(is_head)
+    def _():
+        pl.semaphore_wait(ready_sem, 1)
+
+        @pl.when(odd == 1)
+        def _():
+            start_all(image_ref, late, second_sem, behind, 0)
+
+        @pl.when(odd == 0)
+        def _():
+            @pl.when(me != 0)
+            def _():
+                start_all(image_ref, first, first_sem, behind)
+
+            for index, where in enumerate(pieces):
+                send(first, first, first_sem, where, other).wait_recv()
+                send(first, late, passed_sem, where, other, 1).start()
+                if index == HEAD_START:
+
+                    @pl.when(me == 0)
+                    def _():
+                        start_all(image_ref, first, first_sem, behind)
 
     def turn(index, narrow):
         where = span(index, narrow)
         here = where[0]
         onward = send(first, late, passed_sem, where, other, 1)
-        send(first, first, first_sem, where, other).wait_recv()
-        onward.start()
+
+        @pl.when(jnp.logical_not(even_head))
+        def _():
+            send(first, first, first_sem, where, other).wait_recv()
+            onward.start()
+
         add(even, first[here])
         onward.wait_recv()
         send(own.at[0], late, second_sem, where, other, 0).wait_recv()
         add(odd, late[pl.ds(2 * here.start, 2 * here.size)])
 
-    pl.loop(0, wide)(lambda c: turn(c, False))
+    @pl.loop(0, wide)
+    def _(c):
+        turn(c, False)
     for c in range(TAIL):
         turn(c, True)
 
     to_other.wait_send()
+
+    @pl.when(jnp.logical_not(started))
+    def _():
+        send(own.at[0], first, first_sem, pieces[0], other).wait_send()
+
+    for chosen, (piece, there) in zip(is_relay, RELAYS):
+
+        @pl.when(chosen)
+        def _(piece=piece, there=there):
+            from_relay(piece, there).wait_send()
+
     for where in pieces[1:]:
         send(own.at[0], first, first_sem, where, other).wait_send()
     for where in pieces:
@@ -240,12 +377,15 @@
             pltpu.VMEM((2, rows, depth), jnp.bfloat16),
             block,
             block,
+            pltpu.VMEM((WIDE, depth), jnp.bfloat16),
             pltpu.VMEM((2 * rows, depth), jnp.bfloat16),
             pltpu.SemaphoreType.DMA((2,)),
             pltpu.SemaphoreType.DMA((2,)),
             pair,
             pair,
             pair,
+            pltpu.SemaphoreType.DMA((2,)),
+            pltpu.SemaphoreType.REGULAR,
             pltpu.SemaphoreType.REGULAR,
         ],
         compiler_params=pltpu.CompilerParams(

time: 49.6 us -> 43.3 us (0.87)
  the two profiles are of different devices: /device:TPU:1 before, /device:TPU:6 now
where the time goes in v3:
time: 43.3 us; the launch traced here: 43.1 us
  Pallas kernels  41.2 us (95%)
  between operations  1.93 us (4%)
    pallas_call x1, Pallas kernels, per_device(): pl.pallas_call(lambda *refs: exchange_kernel(count, *refs), out_shape=(pl...  39.4 us
    pallas_call x1, Pallas kernels, per_device(): pl.pallas_call(finish_kernel, out_shape=(jax.ShapeDtypeStruct((rows, dept...  1.79 us

profile of v3, /device:TPU:6, one launch (start us, length us, event | category | flops | bytes accessed | tf_op | source)
XLA Modules:
  0.0 43.1 jit_solution(10526708117379428165)
XLA Ops:
  1.9 39.4 %shard_map.67 = (f32[2,512,1152]{2,1,0:T(8,128)S(1)}, f32[2,512,128]{2,1,0:T(8,128)S(1)}, f32[2,512,128]{2,1,0:T(8,128)S(1)}) custom-call(f32[1]{0:T(128)S(6)} %copy.7.refs_0_, f32[1]{0:T(128)S(6)} %copy.8.refs_1_, bf16[512,1152]{1,0:T(8,128)(2,1)} %refs_2_.1, bf16[512,1152]{1,0:T(8,128)(2,1)} %refs_3_.1), custom_call_target="tpu_custom_call" | custom-call | flops 6643777536 | bytes 4718592 | tf_op jit(solution)/shard_map/pallas_call | solution.py:366
  41.4 1.8 %shard_map.68 = (bf16[512,1152]{1,0:T(8,128)(2,1)}, bf16[512,1152]{1,0:T(8,128)(2,1)}, f32[512]{0:T(512)}) custom-call(f32[2,512,1152]{2,1,0:T(8,128)S(1)} %get-tuple-element.6.total, f32[2,512,128]{2,1,0:T(8,128)S(1)} %get-tuple-element.7.logs, f32[2,512,128]{2,1,0:T(8,128)S(1)} %get-tuple-element.8.lins), custom_call_target="tpu_custom_call" | custom-call | tf_op jit(solution)/shard_map/pallas_call | solution.py:398

commit v4 on v3

--- a/solution.py
+++ b/solution.py
@@ -7,9 +7,10 @@
 
 MESH = pl.DeviceIdType.MESH
 WIDE, NARROW, TAIL = 128, 64, 2
-PIECES = 16
+PIECES = 4
 PLANE = 128
 RELAYS = ((0, 104), (1, 112))
+KEEPERS = ((3, 14), (4, 22))
 HEAD_START = 1
 LOG2E = 1.4426950408889634
 
@@ -36,6 +37,7 @@
     relay_sem,
     ready_sem,
     other_sem,
+    keeper_sem,
 ):
     rows, depth = image_ref.shape
     wide = (rows - NARROW * TAIL) // WIDE
@@ -52,12 +54,17 @@
     even_head = place == 0
     even_tail = place == PLANE - 2
     is_relay = [place == there for _, there in RELAYS]
+    is_keeper = [place == there for _, there in KEEPERS]
 
     def tell(semaphore, device):
         pl.semaphore_signal(semaphore, inc=1, device_id=(device,), device_id_type=MESH)
 
     barrier = pltpu.get_barrier_semaphore()
     tell(barrier, behind)
+
+    @pl.when(place < PLANE - 4)
+    def _():
+        tell(barrier, ahead)
 
     @pl.when(odd == 1)
     def _():
@@ -74,8 +81,17 @@
         def _(there=there):
             tell(barrier, me - there + PLANE - 2)
 
-    heard = 1 + even + jnp.where(even_tail, len(RELAYS), 0)
+    for chosen, (_, there) in zip(is_keeper, KEEPERS):
+
+        @pl.when(chosen)
+        def _(there=there):
+            tell(barrier, me - there)
+            tell(barrier, lax.rem(me - there - 2 + count, count))
+
+    by_ready = jnp.logical_or(is_head, is_tail)
+    heard = 1 + even + jnp.where(by_ready, 0, 1) + jnp.where(even_tail, len(RELAYS), 0)
     heard += sum(jnp.where(chosen, 1, 0) for chosen in is_relay)
+    heard += jnp.where(jnp.logical_or(even_head, even_tail), len(KEEPERS), 0)
 
     loads = []
     for side, ref in ((0, image_ref), (1, text_ref)):
@@ -134,6 +150,35 @@
             device_id_type=MESH,
         )
 
+    def to_keeper(piece, there):
+        here, index = pieces[piece]
+        return pltpu.make_async_remote_copy(
+            src_ref=image_ref.at[here],
+            dst_ref=relayed.at[pl.ds(0, here.size)],
+            send_sem=first_sem.at[0, index],
+            recv_sem=relay_sem.at[1],
+            device_id=(me + there,),
+            device_id_type=MESH,
+        )
+
+    def from_keeper(piece, there):
+        here, index = pieces[piece]
+        return pltpu.make_async_remote_copy(
+            src_ref=relayed.at[pl.ds(0, here.size)],
+            dst_ref=first.at[here],
+            send_sem=relay_sem.at[0],
+            recv_sem=first_sem.at[1, index],
+            device_id=(lax.rem(me - there - 2 + count, count),),
+            device_id_type=MESH,
+        )
+
+    kept = [index for index, _ in KEEPERS]
+
+    def start_unkept():
+        for piece, where in enumerate(pieces):
+            if piece not in kept:
+                send(image_ref, first, first_sem, where, behind).start()
+
     to_other = pltpu.make_async_remote_copy(
         src_ref=own.at[even],
         dst_ref=early,
@@ -144,7 +189,11 @@
     )
 
     pl.semaphore_wait(barrier, heard)
-    tell(ready_sem, ahead)
+
+    @pl.when(place >= PLANE - 4)
+    def _():
+        tell(ready_sem, ahead)
+
 
     neither = jnp.logical_and(place > 0, place < PLANE - 2)
     early_ready = jnp.logical_not(is_head)
@@ -155,12 +204,16 @@
 
     @pl.when(even_head)
     def _():
+        for piece, there in KEEPERS:
+            to_keeper(piece, there).start()
         start_all(text_ref, late, second_sem, ahead, 0)
 
     @pl.when(even_tail)
     def _():
         for piece, there in RELAYS:
             to_relay(piece, there).start()
+        for _, there in KEEPERS:
+            tell(keeper_sem, lax.rem(me + 2 + there, count))
 
     @pl.when(odd == 0)
     def _():
@@ -172,7 +225,10 @@
 
     @pl.when(jnp.logical_and(even == 1, early_ready))
     def _():
-        pl.semaphore_wait(ready_sem, 1)
+        @pl.when(is_tail)
+        def _():
+            pl.semaphore_wait(ready_sem, 1)
+
         start_all(image_ref, first, first_sem, behind)
 
     for load in loads:
@@ -248,7 +304,10 @@
 
     @pl.when(jnp.logical_and(odd == 1, early_ready))
     def _():
-        pl.semaphore_wait(ready_sem, 1)
+        @pl.when(is_tail)
+        def _():
+            pl.semaphore_wait(ready_sem, 1)
+
         start_all(image_ref, late, second_sem, behind, 0)
 
     @pl.when(jnp.logical_and(even == 1, neither))
@@ -274,6 +333,12 @@
             if piece not in [index for index, _ in RELAYS]:
                 send(text_ref, late, second_sem, where, ahead, 0).start()
 
+    def front(index, narrow):
+        where = span(index, narrow)
+        send(first, first, first_sem, where, other).wait_recv()
+        send(first, late, passed_sem, where, other, 1).start()
+        add(even, first[where[0]])
+
     @pl.when(is_head)
     def _():
         pl.semaphore_wait(ready_sem, 1)
@@ -286,35 +351,42 @@
         def _():
             @pl.when(me != 0)
             def _():
-                start_all(image_ref, first, first_sem, behind)
-
-            for index, where in enumerate(pieces):
-                send(first, first, first_sem, where, other).wait_recv()
-                send(first, late, passed_sem, where, other, 1).start()
-                if index == HEAD_START:
-
-                    @pl.when(me == 0)
-                    def _():
-                        start_all(image_ref, first, first_sem, behind)
+                start_unkept()
+
+            @pl.loop(0, wide)
+            def _(c):
+                front(c, False)
+
+                @pl.when(jnp.logical_and(me == 0, c == HEAD_START))
+                def _():
+                    start_unkept()
+
+            for c in range(TAIL):
+                front(c, True)
 
     def turn(index, narrow):
         where = span(index, narrow)
         here = where[0]
-        onward = send(first, late, passed_sem, where, other, 1)
 
         @pl.when(jnp.logical_not(even_head))
         def _():
-            send(first, first, first_sem, where, other).wait_recv()
-            onward.start()
-
-        add(even, first[here])
-        onward.wait_recv()
+            front(index, narrow)
+
+        send(first, late, passed_sem, where, other, 1).wait_recv()
         send(own.at[0], late, second_sem, where, other, 0).wait_recv()
         add(odd, late[pl.ds(2 * here.start, 2 * here.size)])
 
     @pl.loop(0, wide)
     def _(c):
         turn(c, False)
+        for chosen, (piece, there) in zip(is_keeper, KEEPERS):
+
+            @pl.when(jnp.logical_and(chosen, c == 1))
+            def _(piece=piece, there=there):
+                to_keeper(piece, there).wait_recv()
+                pl.semaphore_wait(keeper_sem, 1)
+                from_keeper(piece, there).start()
+
     for c in range(TAIL):
         turn(c, True)
 
@@ -329,6 +401,12 @@
         @pl.when(chosen)
         def _(piece=piece, there=there):
             from_relay(piece, there).wait_send()
+
+    for chosen, (piece, there) in zip(is_keeper, KEEPERS):
+
+        @pl.when(chosen)
+        def _(piece=piece, there=there):
+            from_keeper(piece, there).wait_send()
 
     for where in pieces[1:]:
         send(own.at[0], first, first_sem, where, other).wait_send()
@@ -387,6 +465,7 @@
             pltpu.SemaphoreType.DMA((2,)),
             pltpu.SemaphoreType.REGULAR,
             pltpu.SemaphoreType.REGULAR,
+            pltpu.SemaphoreType.REGULAR,
         ],
         compiler_params=pltpu.CompilerParams(
             collective_id=0, has_side_effects=True, vmem_limit_bytes=40 << 20

time: 43.3 us -> 41.9 us (0.968)
  the two profiles are of different devices: /device:TPU:6 before, /device:TPU:1 now
where the time goes in v4:
time: 41.9 us; the launch traced here: 41.6 us
  Pallas kernels  39.7 us (95%)
  between operations  1.93 us (5%)
    pallas_call x1, Pallas kernels, per_device(): pl.pallas_call(lambda *refs: exchange_kernel(count, *refs), out_shape=(pl...  38.1 us
    pallas_call x1, Pallas kernels, per_device(): pl.pallas_call(finish_kernel, out_shape=(jax.ShapeDtypeStruct((rows, dept...  1.6 us

profile of v4, /device:TPU:1, one launch (start us, length us, event | category | flops | bytes accessed | tf_op | source)
XLA Modules:
  0.0 41.6 jit_solution(8740258191042877725)
XLA Ops:
  1.9 38.1 %shard_map.67 = (f32[2,512,1152]{2,1,0:T(8,128)S(1)}, f32[2,512,128]{2,1,0:T(8,128)S(1)}, f32[2,512,128]{2,1,0:T(8,128)S(1)}) custom-call(f32[1]{0:T(128)S(6)} %copy.7.refs_0_, f32[1]{0:T(128)S(6)} %copy.8.refs_1_, bf16[512,1152]{1,0:T(8,128)(2,1)} %refs_2_.1, bf16[512,1152]{1,0:T(8,128)(2,1)} %refs_3_.1), custom_call_target="tpu_custom_call" | custom-call | flops 6643777536 | bytes 4718592 | tf_op jit(solution)/shard_map/pallas_call | solution.py:444
  40.0 1.6 %shard_map.68 = (bf16[512,1152]{1,0:T(8,128)(2,1)}, bf16[512,1152]{1,0:T(8,128)(2,1)}, f32[512]{0:T(512)}) custom-call(f32[2,512,1152]{2,1,0:T(8,128)S(1)} %get-tuple-element.6.total, f32[2,512,128]{2,1,0:T(8,128)S(1)} %get-tuple-element.7.logs, f32[2,512,128]{2,1,0:T(8,128)S(1)} %get-tuple-element.8.lins), custom_call_target="tpu_custom_call" | custom-call | tf_op jit(solution)/shard_map/pallas_call | solution.py:477

commit v5 on v4

--- a/solution.py
+++ b/solution.py
@@ -6,11 +6,11 @@
 from jax.sharding import PartitionSpec as P
 
 MESH = pl.DeviceIdType.MESH
-WIDE, NARROW, TAIL = 128, 64, 2
+WIDE, NARROW, TAIL = 128, 64, 4
 PIECES = 4
 PLANE = 128
 RELAYS = ((0, 104), (1, 112))
-KEEPERS = ((3, 14), (4, 22))
+KEEPERS = ((2, 14), (3, 22), (4, 38), (5, 46))
 HEAD_START = 1
 LOG2E = 1.4426950408889634
 

time: 41.9 us -> 43.7 us (1.043)
  the two profiles are of different devices: /device:TPU:1 before, /device:TPU:511 now
where the time goes in v5:
time: 43.7 us; the launch traced here: 43.5 us
  Pallas kernels  41.6 us (95%)
  between operations  1.93 us (4%)
    pallas_call x1, Pallas kernels, per_device(): pl.pallas_call(lambda *refs: exchange_kernel(count, *refs), out_shape=(pl...  40 us
    pallas_call x1, Pallas kernels, per_device(): pl.pallas_call(finish_kernel, out_shape=(jax.ShapeDtypeStruct((rows, dept...  1.6 us

profile of v5, /device:TPU:511, one launch (start us, length us, event | category | flops | bytes accessed | tf_op | source)
XLA Modules:
  0.0 43.5 jit_solution(13658785643715301898)
XLA Ops:
  1.9 40.0 %shard_map.67 = (f32[2,512,1152]{2,1,0:T(8,128)S(1)}, f32[2,512,128]{2,1,0:T(8,128)S(1)}, f32[2,512,128]{2,1,0:T(8,128)S(1)}) custom-call(f32[1]{0:T(128)S(6)} %copy.7.refs_0_, f32[1]{0:T(128)S(6)} %copy.8.refs_1_, bf16[512,1152]{1,0:T(8,128)(2,1)} %refs_2_.1, bf16[512,1152]{1,0:T(8,128)(2,1)} %refs_3_.1), custom_call_target="tpu_custom_call" | custom-call | flops 6643777536 | bytes 4718592 | tf_op jit(solution)/shard_map/pallas_call | solution.py:444
  41.9 1.6 %shard_map.68 = (bf16[512,1152]{1,0:T(8,128)(2,1)}, bf16[512,1152]{1,0:T(8,128)(2,1)}, f32[512]{0:T(512)}) custom-call(f32[2,512,1152]{2,1,0:T(8,128)S(1)} %get-tuple-element.6.total, f32[2,512,128]{2,1,0:T(8,128)S(1)} %get-tuple-element.7.logs, f32[2,512,128]{2,1,0:T(8,128)S(1)} %get-tuple-element.8.lins), custom_call_target="tpu_custom_call" | custom-call | tf_op jit(solution)/shard_map/pallas_call | solution.py:477
